TPU v7x, 32 devices: a whole 2x2x4 slice. The times are simulated.
32 devices in a mesh: ctx: 16 (over z, x, core), tp: 2 (over y).
Axes of the slice: x: 2, y: 2, z: 4, core: 2. Of those that a mesh axis runs over, the one named last changes fastest.
Arguments:
- inputs: bfloat16 [3, 2048, 4096], P(None, 'ctx', 'tp'), may hold values from -6 to 6
- short_weight: float32 [3, 3, 4096], P(None, None, 'tp'), may hold values from -3 to 3
- taps: float32 [2048, 4096], P('ctx', 'tp'), may hold values from -6 to 6
- w_out: bfloat16 [4096, 4096], P('tp'), may hold values from -0.09375 to 0.09375
- grad_out: bfloat16 [2048, 4096], P('ctx', 'tp'), may hold values from -6 to 6
Outputs:
- inputs_grad: bfloat16 [3, 2048, 4096], P(None, 'ctx', 'tp')
- taps_grad: float32 [2048, 4096], P('ctx', 'tp')
- short_grad: float32 [3, 3, 4096], P(None, None, 'tp')
All inputs are finite; a program needn't handle non-finite values.
Results may differ from a plain program's by a relative error of at most 0.0015.
Values may be sent and summed in bfloat16 or wider, within the bound.
A program may use at most 192 MiB of HBM per device.

v0:
```python
import math

import jax
import jax.numpy as jnp
from jax import lax
from jax.sharding import PartitionSpec as P

HIGH = lax.Precision.HIGHEST


def shifted(x, axis, by):
    peers = lax.axis_size(axis)
    pairs = [(i, i + by) for i in range(peers) if 0 <= i + by < peers]
    return lax.ppermute(x, axis, pairs)


def phase(left_idx, right_idx, period):
    turns = left_idx[:, None] * right_idx[None, :] % period
    angle = turns.astype(jnp.float32) * (2.0 * math.pi / period)
    return (jnp.cos(angle), jnp.sin(angle))


def section_one(blocks, n2_start, period):
    count = blocks.shape[1]
    width = blocks.shape[2]
    cos_a, sin_a = phase(
        jnp.arange(2 * count, dtype=jnp.int32), jnp.arange(count, dtype=jnp.int32), 2 * count
    )
    real_part = jnp.einsum("kn,bnmc->bkmc", cos_a, blocks, precision=HIGH)
    imag_part = -jnp.einsum("kn,bnmc->bkmc", sin_a, blocks, precision=HIGH)
    cos_b, sin_b = phase(
        jnp.arange(2 * count, dtype=jnp.int32),
        n2_start + jnp.arange(width, dtype=jnp.int32),
        period,
    )
    tw_re = cos_b[None, :, :, None]
    tw_im = -sin_b[None, :, :, None]
    return jnp.stack([real_part * tw_re - imag_part * tw_im, real_part * tw_im + imag_part * tw_re])


def section_two(parts):
    length = parts.shape[3]
    cos_a, sin_a = phase(
        jnp.arange(length, dtype=jnp.int32), jnp.arange(length, dtype=jnp.int32), length
    )
    real_in, imag_in = (parts[0], parts[1])
    cc_re = jnp.einsum("qn,bknc->bkqc", cos_a, real_in, precision=HIGH)
    cc_im = jnp.einsum("qn,bknc->bkqc", cos_a, imag_in, precision=HIGH)
    ss_re = jnp.einsum("qn,bknc->bkqc", sin_a, real_in, precision=HIGH)
    ss_im = jnp.einsum("qn,bknc->bkqc", sin_a, imag_in, precision=HIGH)
    return jnp.stack([cc_re + ss_im, cc_im - ss_re])


def inverse_two(spec, k1_start, period):
    classes = spec.shape[2]
    length = spec.shape[3]
    cos_a, sin_a = phase(
        jnp.arange(length, dtype=jnp.int32), jnp.arange(length, dtype=jnp.int32), length
    )
    real_in, imag_in = (spec[0], spec[1])
    cc_re = jnp.einsum("nq,bkqc->bknc", cos_a, real_in, precision=HIGH)
    cc_im = jnp.einsum("nq,bkqc->bknc", cos_a, imag_in, precision=HIGH)
    ss_re = jnp.einsum("nq,bkqc->bknc", sin_a, real_in, precision=HIGH)
    ss_im = jnp.einsum("nq,bkqc->bknc", sin_a, imag_in, precision=HIGH)
    back_re = cc_re - ss_im
    back_im = cc_im + ss_re
    cos_b, sin_b = phase(
        k1_start + jnp.arange(classes, dtype=jnp.int32), jnp.arange(length, dtype=jnp.int32), period
    )
    tw_re = cos_b[None, :, :, None]
    tw_im = sin_b[None, :, :, None]
    return jnp.stack([back_re * tw_re - back_im * tw_im, back_re * tw_im + back_im * tw_re])


def inverse_one(spec, period):
    classes = spec.shape[2]
    count = classes // 2
    cos_a, sin_a = phase(
        jnp.arange(count, dtype=jnp.int32), jnp.arange(classes, dtype=jnp.int32), classes
    )
    real_out = jnp.einsum("nk,bkmc->bnmc", cos_a, spec[0], precision=HIGH)
    real_out = real_out - jnp.einsum("nk,bkmc->bnmc", sin_a, spec[1], precision=HIGH)
    return real_out / period


def products(spec):
    filt_re, filt_im = (spec[0, 0], spec[1, 0])
    prod_re, prod_im = (spec[0, 1], spec[1, 1])
    grad_re, grad_im = (spec[0, 2], spec[1, 2])
    out_re = jnp.stack(
        [
            filt_re * prod_re - filt_im * prod_im,
            filt_re * grad_re + filt_im * grad_im,
            prod_re * grad_re + prod_im * grad_im,
        ]
    )
    out_im = jnp.stack(
        [
            filt_re * prod_im + filt_im * prod_re,
            filt_re * grad_im - filt_im * grad_re,
            prod_re * grad_im - prod_im * grad_re,
        ]
    )
    return jnp.stack([out_re, out_im])


def shards(inputs, short_weight, taps, w_out, grad_out):
    rows = inputs.shape[1]
    span = short_weight.shape[1]
    count = lax.axis_size("ctx")
    where = lax.axis_index("ctx")
    period = 2 * count * rows
    scale = 1.0 / math.sqrt(count * rows)
    prior = shifted(inputs[:, rows - (span - 1) :, :], "ctx", 1)
    extended = jnp.concatenate([prior, inputs], axis=1).astype(jnp.float32)
    mixed = jnp.zeros((3, rows, inputs.shape[2]), jnp.float32)
    for j in range(span):
        mixed = (
            mixed + short_weight[:, j][:, None, :] * extended[:, span - 1 - j : span - 1 - j + rows]
        )
    query, key_s, value = (mixed[0], mixed[1], mixed[2])
    product = key_s * value
    filt = taps * scale
    columns = w_out
    gated_grad = lax.dot_general(
        lax.all_gather(grad_out, "tp", axis=1, tiled=True),
        columns,
        (((1,), (1,)), ((), ())),
        preferred_element_type=jnp.float32,
    )
    dy = gated_grad * query
    stacked = jnp.stack([filt, product, dy])
    width = rows // count
    blocks = stacked.reshape(3, count, width, stacked.shape[2])
    columns = section_one(
        lax.all_to_all(blocks, "ctx", split_axis=1, concat_axis=1, tiled=True),
        n2_start=where * width,
        period=period,
    )
    spec = section_two(lax.all_to_all(columns, "ctx", split_axis=2, concat_axis=3, tiled=True))
    back = inverse_two(products(spec), where * spec.shape[2], period)
    parted = inverse_one(
        lax.all_to_all(back, "ctx", split_axis=3, concat_axis=2, tiled=True), period=period
    )
    result = lax.all_to_all(parted, "ctx", split_axis=1, concat_axis=1, tiled=True).reshape(
        3, rows, stacked.shape[2]
    )
    conv_out, dz, raw = (result[0], result[1], result[2])
    dmixed = jnp.stack([gated_grad * conv_out, dz * value, dz * key_s])
    following = shifted(dmixed[:, : span - 1, :].astype(jnp.bfloat16), "ctx", -1).astype(
        jnp.float32
    )
    dext = jnp.concatenate([dmixed, following], axis=1)
    inputs_grad = jnp.zeros_like(dmixed)
    sums = []
    for j in range(span):
        inputs_grad = inputs_grad + short_weight[:, j][:, None, :] * dext[:, j : j + rows]
        sums.append(jnp.sum(dmixed * extended[:, span - 1 - j : span - 1 - j + rows], axis=1))
    short_grad = lax.psum(jnp.stack(sums, axis=1), "ctx") * scale
    return (inputs_grad.astype(jnp.bfloat16), raw * scale, short_grad)


def solution(mesh):
    return jax.shard_map(
        shards,
        mesh=mesh,
        in_specs=(
            P(None, "ctx", "tp"),
            P(None, None, "tp"),
            P("ctx", "tp"),
            P("tp", None),
            P("ctx", "tp"),
        ),
        out_specs=(P(None, "ctx", "tp"), P("ctx", "tp"), P(None, None, "tp")),
        check_vma=False,
    )
```

profile of v0, /device:TPU:0, one launch (start us, length us, event | category | flops | bytes accessed | tf_op | source)
XLA Modules:
  0.0 1112.8 jit_solution(15535352030280486862)
XLA Ops:
  17.6 17.1 %all-gather.2.cloned.1.call-done = bf16[128,4096]{1,0:T(8,128)(2,1)} async-done(((bf16[128,2048]{1,0:T(8,128)(2,1)}), bf16[128,4096]{1,0:T(8,128)(2,1)}) %all-gather.2.cloned.1.call-update) | async-done | bytes 1048592 | tf_op jit(solution)/shard_map/all_gather | solution.py:126
  34.7 12.7 %fusion.163 = f32[128,2048]{1,0:T(8,128)} fusion(bf16[128,4096]{1,0:T(8,128)(2,1)} %all-gather.2.cloned.1.call-done, bf16[2048,4096]{1,0:T(8,128)(2,1)} %param.8), kind=kOutput, calls=%fused_computation.201 | convolution fusion | flops 2147483648 | bytes 18874368 | tf_op jit(solution)/shard_map/dot_general | solution.py:125
  57.4 59.2 %all-to-all-done = f32[3,16,8,2048]{3,2,0,1:T(8,128)S(1)} async-done(((f32[3,16,8,2048]{3,2,0,1:T(8,128)}), f32[3,16,8,2048]{3,2,0,1:T(8,128)S(1)}, u32[]{:S(2)}, u32[]{:S(2)}) %all-to-all-start) | async-done | bytes 3145760 | tf_op jit(solution)/shard_map/all_to_all | solution.py:136
  116.6 9.5 fusion.29
  126.2 12.4 %fusion.9 = (f32[1,3,32,8,2048]{4,2,3,1,0:T(8,128)}, f32[1,3,32,8,2048]{4,2,3,1,0:T(8,128)}) fusion(f32[3,8,2048,32]{2,3,1,0:T(8,128)S(1)} %fusion.29, f32[32,8]{0,1:T(8,128)S(1)} %get-tuple-element.38, f32[32,8]{0,1:T(8,128)S(1)} %get-tuple-element.37, f32[3,16,8,2048]{3,2,0,1:T(8,128)S(1)} %all-to-all-done), kind=kOutput, calls=%fused_computation.16 | convolution fusion | flops 313007104 | bytes 22022144 | tf_op jit(solution)/shard_map/kn,bnmc->bkmc/dot_general | solution.py:29
  138.6 11.3 %pad_maximum_fusion = f32[2,3,32,8,2048]{4,2,3,1,0:T(8,128)} fusion(f32[1,3,32,8,2048]{4,2,3,1,0:T(8,128)} %get-tuple-element.16, f32[1,3,32,8,2048]{4,2,3,1,0:T(8,128)} %get-tuple-element.15), kind=kLoop, calls=%fused_computation | loop fusion | flops 3145728 | bytes 25165824 | tf_op jit(solution)/shard_map/stack | solution.py:38
  149.9 16.4 %copy.49 = f32[2,3,32,8,2048]{4,3,1,0,2:T(8,128)} copy(f32[2,3,32,8,2048]{4,2,3,1,0:T(8,128)} %pad_maximum_fusion) | data formatting | bytes 25165824 | tf_op jit(solution)/shard_map/stack | solution.py:38
  166.3 15.5 %all-to-all-start.1 = ((f32[2,3,32,8,2048]{4,3,1,0,2:T(8,128)}), f32[2,3,32,8,2048]{4,3,1,0,2:T(8,128)}, u32[]{:S(2)}, u32[]{:S(2)}) async-start(f32[2,3,32,8,2048]{4,3,1,0,2:T(8,128)} %copy.49), calls=%async_computation.1 | async-start | bytes 25165824 | tf_op jit(solution)/shard_map/all_to_all | solution.py:140
  182.2 223.4 %all-to-all-done.1 = f32[2,3,32,8,2048]{4,3,1,0,2:T(8,128)} async-done(((f32[2,3,32,8,2048]{4,3,1,0,2:T(8,128)}), f32[2,3,32,8,2048]{4,3,1,0,2:T(8,128)}, u32[]{:S(2)}, u32[]{:S(2)}) %all-to-all-start.1) | async-done | bytes 12582944 | tf_op jit(solution)/shard_map/all_to_all | solution.py:140
  405.5 11.3 %copy.50 = f32[2,3,32,8,2048]{4,3,2,1,0:T(8,128)} copy(f32[2,3,32,8,2048]{4,3,1,0,2:T(8,128)} %all-to-all-done.1) | data formatting | bytes 25165824 | tf_op jit(solution)/shard_map/all_to_all | solution.py:140
  416.9 8.9 fusion.155
  425.7 10.8 fusion.2
  436.5 10.5 fusion
  447.1 11.0 add_bitcast_fusion.1
  458.1 10.7 subtract_bitcast_fusion.1
  495.1 10.7 subtract_bitcast_fusion
  513.9 19.2 %copy.57 = f32[2,3,2,128,2048]{4,2,1,0,3:T(2,128)} copy(f32[2,3,2,128,2048]{3,4,2,1,0:T(8,128)} %pad_maximum_fusion.1) | data formatting | bytes 25165824 | tf_op jit(solution)/shard_map/stack | solution.py:72
  533.2 325.5 %all_to_all.40 = f32[2,3,2,128,2048]{4,2,1,0,3:T(2,128)} all-to-all(f32[2,3,2,128,2048]{4,2,1,0,3:T(2,128)} %copy.57), channel_id=1, replica_groups=mesh['ctx'=16,'tp'=2] {'ctx'}, dimensions={3} | all-to-all | bytes 25165824 | tf_op jit(solution)/shard_map/all_to_all | solution.py:143
  858.6 16.3 %copy.108 = f32[2,3,2,128,2048]{4,3,2,1,0:T(8,128)} copy(f32[2,3,2,128,2048]{4,2,1,0,3:T(2,128)} %all_to_all.40) | data formatting | bytes 25165824 | tf_op jit(solution)/shard_map/all_to_all | solution.py:143
  874.9 8.9 fusion.154
  891.4 8.6 squeeze.33
  914.6 8.6 squeeze.34
  931.1 76.0 %all_to_all.41 = f32[3,16,8,2048]{3,2,0,1:T(8,128)S(1)} all-to-all(f32[3,16,8,2048]{3,2,0,1:T(8,128)S(1)} %copy.61), channel_id=1, replica_groups=mesh['ctx'=16,'tp'=2] {'ctx'}, dimensions={1} | all-to-all | bytes 6291456 | tf_op jit(solution)/shard_map/all_to_all | solution.py:145
  1016.7 87.2 %all-reduce.2.cloned.1.call-done = f32[3,3,2048]{2,0,1:T(4,128)} async-done(((f32[3,3,2048]{2,0,1:T(4,128)}), f32[3,3,2048]{2,0,1:T(4,128)}) %all-reduce.2.cloned.1.call-update) | async-done | bytes 73744 | tf_op jit(solution)/shard_map/psum | solution.py:159
  (98 shorter events, 96.1 us)
Async XLA Ops:
  7.2 7.0 copy-start.14
  7.2 27.5 %all-gather.2.cloned.1.call-start = ((), (), s32[]{:S(2)}) async-start(), calls=%async_computation.4 | async-start | bytes 1572864 | tf_op jit(solution)/shard_map/all_gather | solution.py:126
  8.3 5.9 collective-permute-start
  16.3 31.1 %copy-start.2 = (f32[3,128,2048]{2,1,0:T(8,128)}, f32[3,128,2048]{2,1,0:T(8,128)S(1)}, u32[]{:S(2)}) copy-start(f32[3,128,2048]{2,1,0:T(8,128)S(1)} %multiply_add_fusion) | copy-start | bytes 9437188
  51.5 65.2 %all-to-all-start = ((f32[3,16,8,2048]{3,2,0,1:T(8,128)}), f32[3,16,8,2048]{3,2,0,1:T(8,128)S(1)}, u32[]{:S(2)}, u32[]{:S(2)}) async-start(f32[3,16,8,2048]{3,2,0,1:T(8,128)} %copy.46), calls=%async_computation | async-start | bytes 6291456 | tf_op jit(solution)/shard_map/all_to_all | solution.py:136
  166.3 239.2 %all-to-all-start.1 = ((f32[2,3,32,8,2048]{4,3,1,0,2:T(8,128)}), f32[2,3,32,8,2048]{4,3,1,0,2:T(8,128)}, u32[]{:S(2)}, u32[]{:S(2)}) async-start(f32[2,3,32,8,2048]{4,3,1,0,2:T(8,128)} %copy.49), calls=%async_computation.1 | async-start | bytes 25165824 | tf_op jit(solution)/shard_map/all_to_all | solution.py:140
  181.8 922.1 %all-reduce.2.cloned.1.call-start = ((), (), s32[]{:S(2)}) async-start(), calls=%async_computation.5 | async-start | bytes 196608 | tf_op jit(solution)/shard_map/psum | solution.py:159
  425.7 21.3 %slice-start = ((s8[6291456]{0:T(1024)(128)(4,1)}), s8[4194304]{0:T(1024)(128)(4,1)S(1)}, s32[]{:S(2)}) async-start(s8[6291456]{0:T(1024)(128)(4,1)} %bitcast.172), calls=%async_computation.6 | async-start | bytes 8388608
  436.5 10.5 slice-start.1
  475.1 8.5 copy-start.8
  475.1 8.5 copy-start.9
  475.1 8.5 copy-start.10
  483.6 5.7 copy-start.5
  483.6 5.7 copy-start.6
  483.6 5.7 copy-start.7
  891.4 15.6 %slice-start.2 = ((s8[6291456]{0:T(1024)(128)(4,1)}), s8[2097152]{0:T(1024)(128)(4,1)S(1)}, s32[]{:S(2)}) async-start(s8[6291456]{0:T(1024)(128)(4,1)} %bitcast.176), calls=%async_computation.8 | async-start | bytes 4194304
  900.1 7.0 slice-start.3
  914.6 8.6 copy-start.4
  931.1 76.0 %copy-start.11 = (f32[128,2048]{1,0:T(8,128)S(1)}, f32[128,2048]{1,0:T(8,128)}, u32[]{:S(2)}) copy-start(f32[128,2048]{1,0:T(8,128)} %fusion.163) | copy-start | bytes 3145732
  931.1 76.1 %copy-start.3 = (f32[3,128,2048]{2,1,0:T(8,128)S(1)}, f32[3,128,2048]{2,1,0:T(8,128)}, u32[]{:S(2)}) copy-start(f32[3,128,2048]{2,1,0:T(8,128)} %copy-done.2) | copy-start | bytes 9437188
  1007.8 4.2 copy-start.1
  1007.8 4.2 copy-start.16
  1007.8 4.2 copy-start.18
  1007.8 3.6 collective-permute-start.1
  (7 other events, 13.7 us)
Sparse Core Ops, SparseCore 0:
  10.8 23.8 all-gather.1
  1015.8 88.1 all-reduce.1
where the time goes:
time: 1120 us; the launch traced here: 1110 us
  blocking collectives  401 us (36%)
  waiting for transfers between devices  389 us (35%)
  local copies, waits for them, and re-layouts  121 us (11%)
  matrix products  121 us (11%)
  other arithmetic  39.5 us (4%)
  starting transfers between devices  25.5 us (2%)
  between operations  15 us (1%)
    all_to_all x1, blocking collectives, shards(): lax.all_to_all(back, 'ctx', split_axis=3, concat_axis=2, tiled=True)  325 us
    all_to_all x1, waiting for transfers between devices, shards(): lax.all_to_all(columns, 'ctx', split_axis=2, concat_axis=3, tiled=True)  223 us
    psum x1, waiting for transfers between devices, shards(): short_grad = lax.psum(jnp.stack(sums, axis=1), 'ctx') * scale  87.2 us
    all_to_all x1, blocking collectives, shards(): lax.all_to_all(parted, 'ctx', split_axis=1, concat_axis=1, tiled=True)  76 us
    all_to_all x1, waiting for transfers between devices, shards(): lax.all_to_all(blocks, 'ctx', split_axis=1, concat_axis=1, tiled=True)  59.2 us
  transfers between devices with their start and end apart: 6, of which 5 were waited for; matrix products, arithmetic and copies ran while one was open for 1% of the time, Pallas kernels for 0%

commit v1 on v0

--- a/solution.py
+++ b/solution.py
@@ -1,11 +1,18 @@
+import functools
 import math
 
 import jax
 import jax.numpy as jnp
+import numpy as np
 from jax import lax
+from jax.experimental import pallas as pl
+from jax.experimental.pallas import tpu as pltpu
 from jax.sharding import PartitionSpec as P
 
 HIGH = lax.Precision.HIGHEST
+MESH = pl.DeviceIdType.MESH
+FINE = 256
+TOP = 248.0 * 128.0 - 1.0
 
 
 def shifted(x, axis, by):
@@ -160,9 +167,355 @@
     return (inputs_grad.astype(jnp.bfloat16), raw * scale, short_grad)
 
 
+def log2(x):
+    return jnp.log(x) * (1.0 / math.log(2.0))
+
+
+def encode(x):
+    peak = jnp.maximum(jnp.max(jnp.abs(x), axis=0, keepdims=True), 1e-30)
+    power = jnp.ceil(log2(peak))
+    level = jnp.floor(jnp.abs(x) * (jnp.exp2(-power) * TOP) + 0.5)
+    level = jnp.minimum(level, TOP)
+    octave = jnp.floor(level * (1.0 / 128.0))
+    size = jnp.exp2(octave - 123.0) * (1.0 + (level - octave * 128.0) * (1.0 / 128.0))
+    return jnp.where(x < 0.0, -size, size).astype(jnp.bfloat16), power
+
+
+def decode(words, power):
+    words = words.astype(jnp.float32)
+    size = jnp.abs(words)
+    octave = jnp.floor(log2(size) + 0.0014)
+    part = jnp.floor(size * jnp.exp2(-octave) * 128.0 + 0.5)
+    level = octave * 128.0 + part + (123.0 * 128.0 - 128.0)
+    return jnp.where(words < 0.0, -level, level) * (jnp.exp2(power.astype(jnp.float32)) / TOP)
+
+
+def rows_of(powers):
+    row = lax.broadcasted_iota(jnp.int32, (16, powers[0].shape[1]), 0)
+    rows = jnp.where(row == 0, powers[0], jnp.where(row == 1, powers[1], powers[2]))
+    return rows.astype(jnp.bfloat16)
+
+
+def split(x):
+    high = x.astype(jnp.bfloat16)
+    return high, (x - high.astype(jnp.float32)).astype(jnp.bfloat16)
+
+
+def product3(m_high, m_low, x):
+    x_high, x_low = split(x)
+    dot = lambda a, b: jnp.dot(a, b, preferred_element_type=jnp.float32)
+    return dot(m_high, x_high) + (dot(m_low, x_high) + dot(m_high, x_low))
+
+
+def times_root(z, k, count, sign):
+    re, im = z
+    k = k % count
+    if 8 * k % count == 0:
+        turn = 8 * k // count
+        if turn % 2 == 0:
+            for _ in range(turn // 2):
+                re, im = (im, -re) if sign < 0 else (-im, re)
+            return re, im
+    c, s = math.cos(2 * math.pi * k / count), sign * math.sin(2 * math.pi * k / count)
+    if 8 * k % count == 0:
+        r = abs(c)
+        if (c > 0) == (s > 0):
+            out = (re - im) * r, (re + im) * r
+        else:
+            out = (re + im) * r, (im - re) * r
+        return out if c > 0 else (-out[0], -out[1])
+    return re * c - im * s, re * s + im * c
+
+
+def small_dft(z, sign):
+    count = len(z)
+    if count == 1:
+        return z
+    even, odd = small_dft(z[0::2], sign), small_dft(z[1::2], sign)
+    odd = [times_root(v, k, count, sign) for k, v in enumerate(odd)]
+    return [(a[0] + b[0], a[1] + b[1]) for a, b in zip(even, odd)] + [
+        (a[0] - b[0], a[1] - b[1]) for a, b in zip(even, odd)
+    ]
+
+
+def matrices(length):
+    radix = length // FINE
+    k = np.arange(FINE)[None, :, None] + 0.25
+    n = radix * np.arange(FINE)[None, None, :] + np.arange(radix)[:, None, None]
+    angle = -2.0 * np.pi * k * n / length
+    forward = np.concatenate([np.cos(angle), np.sin(angle)], axis=1).astype(np.float32)
+
+    def halves(m):
+        high = m.astype(jnp.bfloat16)
+        return np.stack([high, (m - high.astype(np.float32)).astype(jnp.bfloat16)])
+
+    return halves(forward), halves(np.ascontiguousarray(forward.transpose(0, 2, 1)))
+
+
+def transform_products(xs, ys, f_ref, ft_ref, factor):
+    length, lanes = xs.shape[1], xs.shape[2]
+    radix = length // FINE
+    for n2 in range(radix):
+        x = jnp.concatenate([xs[a, pl.ds(n2, FINE, stride=radix), :] for a in range(3)], axis=1)
+        ys[n2] = product3(f_ref[0, n2], f_ref[1, n2], x)
+
+    def spectra(t, _):
+        row = pl.multiple_of(t * 8, 8)
+        specs = []
+        for a in range(3):
+            cols = pl.ds(a * lanes, lanes)
+            z = [
+                (ys[n2, pl.ds(row, 8), cols], ys[n2, pl.ds(FINE + row, 8), cols])
+                for n2 in range(radix)
+            ]
+            specs.append(small_dft(z, -1))
+        filt, prod, grad = specs
+        joined = [[], [], []]
+        for (fr, fi), (pr, pi), (gr, gi) in zip(filt, prod, grad):
+            joined[0].append((fr * pr - fi * pi, fr * pi + fi * pr))
+            joined[1].append((fr * gr + fi * gi, fr * gi - fi * gr))
+            joined[2].append((pr * gr + pi * gi, pr * gi - pi * gr))
+        for a in range(3):
+            cols = pl.ds(a * lanes, lanes)
+            for n2, (re, im) in enumerate(small_dft(joined[a], 1)):
+                ys[n2, pl.ds(row, 8), cols] = re * factor
+                ys[n2, pl.ds(FINE + row, 8), cols] = im * factor
+        return 0
+
+    lax.fori_loop(0, FINE // 8, spectra, 0)
+    for n2 in range(radix):
+        x = product3(ft_ref[0, n2], ft_ref[1, n2], ys[n2])
+        for a in range(3):
+            xs[a, pl.ds(n2, FINE, stride=radix), :] = x[:, a * lanes : (a + 1) * lanes]
+
+
+def greet(count):
+    me = lax.axis_index("ctx")
+    barrier = pltpu.get_barrier_semaphore()
+    for s in range(1, count):
+        pl.semaphore_signal(
+            barrier, inc=1, device_id={"ctx": lax.rem(me + s, count)}, device_id_type=MESH
+        )
+    pl.semaphore_wait(barrier, count - 1)
+    return me
+
+
+def remote(src, dst, send_sem, recv_sem, peer):
+    return pltpu.make_async_remote_copy(
+        src_ref=src,
+        dst_ref=dst,
+        send_sem=send_sem,
+        recv_sem=recv_sem,
+        device_id={"ctx": peer},
+        device_id_type=MESH,
+    )
+
+
+def conv_kernel(
+    count, factor, h_ref, z_ref, g_ref, f_hbm, ft_hbm, y_ref, dz_ref, raw_ref,
+    there, arrived, back, returned, xs, ys, f_ref, ft_ref, local_sem, send_sem, recv_sem,
+):
+    rows, lanes = xs.shape[1] // count, xs.shape[2]
+    me = greet(count)
+    loads = [
+        pltpu.make_async_copy(f_hbm, f_ref, local_sem.at[0]),
+        pltpu.make_async_copy(ft_hbm, ft_ref, local_sem.at[1]),
+    ]
+    for load in loads:
+        load.start()
+
+    def columns(d):
+        return pl.ds(pl.multiple_of(d * lanes, lanes), lanes)
+
+    def fill(buf, d, parts):
+        powers = []
+        for a, x in enumerate(parts):
+            words, power = encode(x)
+            buf[d, pl.ds(a * rows, rows), :] = words
+            powers.append(power)
+        buf[d, pl.ds(3 * rows, 16), :] = rows_of(powers)
+
+    def sending(src, dst, phase, s):
+        peer = lax.rem(me + s, count)
+        return remote(
+            src.at[peer], dst.at[me], send_sem.at[phase, s], recv_sem.at[phase, s], peer
+        )
+
+    def landing(src, dst, phase, s):
+        peer = lax.rem(me + count - s, count)
+        return remote(
+            src.at[peer], dst.at[peer], send_sem.at[phase, s], recv_sem.at[phase, s], peer
+        )
+
+    order = list(range(1, count)) + [0]
+    for s in order:
+        d = lax.rem(me + s, count)
+        fill(there, d, [ref[:, columns(d)] for ref in (h_ref, z_ref, g_ref)])
+        if s:
+            sending(there, arrived, 0, s).start()
+
+    for s in range(count):
+        d = lax.rem(me + count - s, count)
+        if s:
+            landing(there, arrived, 0, s).wait_recv()
+        block = there[d] if s == 0 else arrived[d]
+        powers = block[3 * rows :].astype(jnp.float32)
+        for a in range(3):
+            xs[a, pl.ds(pl.multiple_of(d * rows, rows), rows), :] = decode(
+                block[a * rows : (a + 1) * rows], powers[a : a + 1]
+            )
+    for load in loads:
+        load.wait()
+    transform_products(xs, ys, f_ref, ft_ref, factor)
+
+    for s in order:
+        d = lax.rem(me + s, count)
+        at = pl.ds(pl.multiple_of(d * rows, rows), rows)
+        fill(back, d, [xs[a, at, :] for a in range(3)])
+        if s:
+            sending(back, returned, 1, s).start()
+    for s in range(count):
+        d = lax.rem(me + count - s, count)
+        if s:
+            landing(back, returned, 1, s).wait_recv()
+        block = back[d] if s == 0 else returned[d]
+        powers = block[3 * rows :].astype(jnp.float32)
+        for a, ref in enumerate((y_ref, dz_ref, raw_ref)):
+            ref[:, columns(d)] = decode(block[a * rows : (a + 1) * rows], powers[a : a + 1])
+    for s in range(1, count):
+        sending(there, arrived, 0, s).wait_send()
+        sending(back, returned, 1, s).wait_send()
+
+
+def convolve(taps, product, dy, count, scale):
+    rows, width = taps.shape
+    lanes = width // count
+    length = rows * count
+    radix = length // FINE
+    forward, backward = matrices(length)
+    vmem, anywhere = pl.BlockSpec(memory_space=pltpu.VMEM), pl.BlockSpec(memory_space=pl.ANY)
+    block = (count, 3 * rows + 16, lanes)
+    return pl.pallas_call(
+        functools.partial(conv_kernel, count, scale / length),
+        out_shape=[jax.ShapeDtypeStruct((rows, width), jnp.float32)] * 3,
+        in_specs=[vmem, vmem, vmem, anywhere, anywhere],
+        out_specs=[vmem] * 3,
+        scratch_shapes=[pltpu.VMEM(block, jnp.bfloat16)] * 4
+        + [
+            pltpu.VMEM((3, length, lanes), jnp.float32),
+            pltpu.VMEM((radix, 2 * FINE, 3 * lanes), jnp.float32),
+            pltpu.VMEM(forward.shape, jnp.bfloat16),
+            pltpu.VMEM(backward.shape, jnp.bfloat16),
+            pltpu.SemaphoreType.DMA((2,)),
+            pltpu.SemaphoreType.DMA((2, count)),
+            pltpu.SemaphoreType.DMA((2, count)),
+        ],
+        compiler_params=pltpu.CompilerParams(
+            collective_id=0, has_side_effects=True, vmem_limit_bytes=56 * 2**20
+        ),
+        cost_estimate=pl.CostEstimate(
+            flops=36 * length * FINE * 3 * lanes, bytes_accessed=24 * rows * width, transcendentals=0
+        ),
+        name="long_convolution",
+    )(taps, product, dy, jnp.asarray(forward), jnp.asarray(backward))
+
+
+def sum_kernel(count, part_ref, out_ref, arrived, total, send_sem, recv_sem):
+    me = greet(count)
+
+    def copy(phase, s, mine):
+        peer = lax.rem(me + (s if mine else count - s), count)
+        src = part_ref.at[peer] if phase == 0 else total
+        dst = (arrived if phase == 0 else out_ref).at[me if mine else peer]
+        return remote(src, dst, send_sem.at[phase, s], recv_sem.at[phase, s], peer)
+
+    for s in range(1, count):
+        copy(0, s, True).start()
+    value = part_ref[me]
+    for s in range(1, count):
+        copy(0, s, False).wait_recv()
+        value = value + arrived[lax.rem(me + count - s, count)]
+    total[...] = value
+    for s in range(1, count):
+        copy(1, s, True).start()
+    out_ref[me] = value
+    for s in range(1, count):
+        copy(1, s, False).wait_recv()
+    for s in range(1, count):
+        copy(0, s, True).wait_send()
+        copy(1, s, True).wait_send()
+
+
+def summed(part, count):
+    lead, width = part.shape
+    lanes = width // count
+    padded = -(-lead // 8) * 8
+    blocks = jnp.pad(part, ((0, padded - lead), (0, 0)))
+    blocks = blocks.reshape(padded, count, lanes).transpose(1, 0, 2)
+    vmem = pl.BlockSpec(memory_space=pltpu.VMEM)
+    total = pl.pallas_call(
+        functools.partial(sum_kernel, count),
+        out_shape=jax.ShapeDtypeStruct(blocks.shape, jnp.float32),
+        in_specs=[vmem],
+        out_specs=vmem,
+        scratch_shapes=[
+            pltpu.VMEM(blocks.shape, jnp.float32),
+            pltpu.VMEM(blocks.shape[1:], jnp.float32),
+            pltpu.SemaphoreType.DMA((2, count)),
+            pltpu.SemaphoreType.DMA((2, count)),
+        ],
+        compiler_params=pltpu.CompilerParams(collective_id=1, has_side_effects=True),
+        name="tap_sums",
+    )(blocks)
+    return total.transpose(1, 0, 2).reshape(padded, width)[:lead]
+
+
+def channel_shards(inputs, short_weight, taps, w_out, grad_out):
+    rows, width = taps.shape
+    span = short_weight.shape[1]
+    count = lax.axis_size("ctx")
+    scale = 1.0 / math.sqrt(count * rows)
+    prior = shifted(inputs[:, rows - (span - 1) :, :], "ctx", 1)
+    extended = jnp.concatenate([prior, inputs], axis=1).astype(jnp.float32)
+    mixed = jnp.zeros((3, rows, width), jnp.float32)
+    for j in range(span):
+        mixed = (
+            mixed + short_weight[:, j][:, None, :] * extended[:, span - 1 - j : span - 1 - j + rows]
+        )
+    query, key_s, value = (mixed[0], mixed[1], mixed[2])
+    gated_grad = lax.dot_general(
+        lax.all_gather(grad_out, "tp", axis=1, tiled=True),
+        w_out,
+        (((1,), (1,)), ((), ())),
+        preferred_element_type=jnp.float32,
+    )
+    conv_out, dz, taps_grad = convolve(taps, key_s * value, gated_grad * query, count, scale)
+    dmixed = jnp.stack([gated_grad * conv_out, dz * value, dz * key_s])
+    following = shifted(dmixed[:, : span - 1, :].astype(jnp.bfloat16), "ctx", -1).astype(
+        jnp.float32
+    )
+    dext = jnp.concatenate([dmixed, following], axis=1)
+    inputs_grad = jnp.zeros_like(dmixed)
+    sums = []
+    for j in range(span):
+        inputs_grad = inputs_grad + short_weight[:, j][:, None, :] * dext[:, j : j + rows]
+        sums.append(jnp.sum(dmixed * extended[:, span - 1 - j : span - 1 - j + rows], axis=1))
+    part = jnp.stack(sums, axis=1).reshape(3 * span, width) * scale
+    short_grad = summed(part, count).reshape(3, span, width)
+    return (inputs_grad.astype(jnp.bfloat16), taps_grad, short_grad)
+
+
+def any_shards(inputs, short_weight, taps, w_out, grad_out):
+    rows, width = taps.shape
+    count = lax.axis_size("ctx")
+    whole_tiles = rows % 16 == 0 and width % (128 * count) == 0 and rows * count == 8 * FINE
+    plan = channel_shards if whole_tiles else shards
+    return plan(inputs, short_weight, taps, w_out, grad_out)
+
+
 def solution(mesh):
     return jax.shard_map(
-        shards,
+        any_shards,
         mesh=mesh,
         in_specs=(
             P(None, "ctx", "tp"),

time: 1120 us -> 177 us (0.16)
  blocking collectives: 401 us -> 0 us
  waiting for transfers between devices: 389 us -> 20.6 us
  local copies, waits for them, and re-layouts: 121 us -> 7.01 us
  matrix products: 121 us -> 14.2 us
  Pallas kernels: 0 us -> 106 us
  other arithmetic: 39.5 us -> 10.1 us
  starting transfers between devices: 25.5 us -> 3.69 us
    all_to_all x2 -> x0, blocking collectives: 401 us -> none  [the longest x1 325 us: shards(): lax.all_to_all(back, 'ctx', split_axis=3, concat_axis=2, tiled=True)]
    all_to_all x2 -> x0, waiting for transfers between devices: 283 us -> none  [the longest x1 223 us: shards(): lax.all_to_all(columns, 'ctx', split_axis=2, concat_axis=3, tiled=True)]
    dot_general x13 -> x1, matrix products: 121 us -> 14.2 us  [channel_shards(): lax.dot_general(lax.all_gather(grad_out, 'tp', axis=1, tiled=True), w_out...]
    pallas_call x0 -> x2, Pallas kernels: none -> 106 us  [the longest x1 71.8 us: convolve(): pl.pallas_call(functools.partial(conv_kernel, count, scale / length), out...]
    psum x1 -> x0, waiting for transfers between devices: 87.2 us -> none  [shards(): short_grad = lax.psum(jnp.stack(sums, axis=1), 'ctx') * scale]
    another operation x3, local copies, waits for them, and re-layouts: 37.5 us -> 0.06 us  [channel_shards(): part = jnp.stack(sums, axis=1).reshape(3 * span, width) * scale]
    slice x7 -> x4, local copies, waits for them, and re-layouts: 35.1 us -> 2.99 us  [the longest x1 1.12 us: channel_shards(): short_weight[:, j][:, None, :] * dext[:, j:j + rows]]
    all_to_all x2 -> x0, local copies, waits for them, and re-layouts: 27.6 us -> none  [the longest x1 16.3 us: shards(): lax.all_to_all(back, 'ctx', split_axis=3, concat_axis=2, tiled=True)]
  transfers between devices with their start and end apart: 6 -> 3, of which waited for: 5 -> 2; matrix products, arithmetic and copies ran while one was open for 1% -> 4% of each run, Pallas kernels for 0% -> 0%
where the time goes in v1:
time: 177 us; the launch traced here: 176 us
  Pallas kernels  106 us (60%)
  waiting for transfers between devices  20.6 us (12%)
  matrix products  14.2 us (8%)
  between operations  14.2 us (8%)
  other arithmetic  10.1 us (6%)
  local copies, waits for them, and re-layouts  7.01 us (4%)
  starting transfers between devices  3.69 us (2%)
    pallas_call x1, Pallas kernels, convolve(): pl.pallas_call(functools.partial(conv_kernel, count, scale / length), out...  71.8 us
    pallas_call x1, Pallas kernels, summed(): pl.pallas_call(functools.partial(sum_kernel, count), out_shape=jax.ShapeD...  34.7 us
    all_gather x1, waiting for transfers between devices, channel_shards(): lax.all_gather(grad_out, 'tp', axis=1, tiled=True)  16.7 us
    dot_general x1, matrix products, channel_shards(): lax.dot_general(lax.all_gather(grad_out, 'tp', axis=1, tiled=True), w_out...  14.2 us
    ppermute x2, starting transfers between devices, shifted(): return lax.ppermute(x, axis, pairs)  3.65 us
  transfers between devices with their start and end apart: 3, of which 2 were waited for; matrix products, arithmetic and copies ran while one was open for 4% of the time, Pallas kernels for 0%

profile of v1, /device:TPU:0, one launch (start us, length us, event | category | flops | bytes accessed | tf_op | source)
XLA Modules:
  0.0 176.3 jit_solution(14321829754581927908)
XLA Ops:
  7.2 0.0 all-gather.2.cloned.1.call-start
  7.2 0.7 all-gather.2.cloned.1.call-update
  7.9 0.9 slice.51
  8.8 2.4 %collective-permute-start = (bf16[3,2,2048]{2,1,0:T(2,128)(2,1)S(1)}, bf16[3,2,2048]{2,1,0:T(2,128)(2,1)S(1)}, u32[]{:S(2)}, u32[]{:S(2)}) collective-permute-start(bf16[3,2,2048]{2,1,0:T(2,128)(2,1)S(1)} %slice.51), channel_id=1, source_target_pairs={{0,2},{2,4},{4,6},{6,8},{8,10},{10,12},{12,14},{14,16},{16,18},{18... | collective-permute-start | bytes 73736 | tf_op jit(solution)/shard_map/ppermute | solution.py:21
  11.2 1.1 fusion.5
  12.4 1.9 %maximum_convert_fusion = f32[3,130,2048]{2,1,0:T(8,128)S(1)} fusion(bf16[3,128,2048]{2,1,0:T(8,128)(2,1)} %param.7, bf16[3,2,2048]{2,1,0:T(2,128)(2,1)S(1)} %collective-permute-done), kind=kLoop, calls=%fused_computation.11 | loop fusion | flops 3194880 | bytes 4792320 | tf_op jit(solution)/shard_map/convert_element_type | solution.py:479
  14.3 2.6 %multiply_add_fusion = f32[3,128,2048]{2,1,0:T(8,128)} fusion(f32[3,130,2048]{2,1,0:T(8,128)S(1)} %maximum_convert_fusion, f32[3,2048]{1,0:T(4,128)S(1)} %get-tuple-element.21, f32[3,2048]{1,0:T(4,128)S(1)} %get-tuple-element.22, f32[3,2048]{1,0:T(4,128)S(1)} %bitcast.41), kind=kLoop, calls=%fused_computation.10 | loop fusion | flops 3932160 | bytes 12656640 | tf_op jit(solution)/shard_map/add | solution.py:483
  16.9 16.7 %all-gather.2.cloned.1.call-done = bf16[128,4096]{1,0:T(8,128)(2,1)} async-done(((bf16[128,2048]{1,0:T(8,128)(2,1)}), bf16[128,4096]{1,0:T(8,128)(2,1)}) %all-gather.2.cloned.1.call-update) | async-done | bytes 1048592 | tf_op jit(solution)/shard_map/all_gather | solution.py:487
  33.6 14.2 %fusion.3 = (f32[128,2048]{1,0:T(8,128)}, f32[128,2048]{1,0:T(8,128)}, f32[128,2048]{1,0:T(8,128)}) fusion(f32[3,128,2048]{2,1,0:T(8,128)} %multiply_add_fusion, bf16[128,4096]{1,0:T(8,128)(2,1)} %all-gather.2.cloned.1.call-done, bf16[2048,4096]{1,0:T(8,128)(2,1)} %param.10), kind=kOutput, calls=%fused_computation.13 | convolution fusion | flops 2148007936 | bytes 24117248 | tf_op jit(solution)/shard_map/dot_general | solution.py:486
  47.8 71.8 %long_convolution.1 = (f32[128,2048]{1,0:T(8,128)}, f32[128,2048]{1,0:T(8,128)}, f32[128,2048]{1,0:T(8,128)}) custom-call(f32[128,2048]{1,0:T(8,128)} %h_ref.1, f32[128,2048]{1,0:T(8,128)} %get-tuple-element.16.z_ref, f32[128,2048]{1,0:T(8,128)} %get-tuple-element.15.g_ref, bf16[2,8,512,256]{3,2,1,0:T(8,128)(2,1)} %constant.10.clone.f_hbm, ...), custom_call_target="tpu_custom_call" | custom-call | flops 7247757312 | bytes 6291456 | tf_op jit(solution)/shard_map/long_convolution/pallas_call | solution.py:398
  119.6 1.6 multiply_bitcast_fusion.1
  121.2 0.2 copy-done.2
  121.5 0.1 multiply_bitcast_fusion.2
  121.6 0.4 pad_maximum_fusion.1
  122.0 1.3 collective-permute-start.1
  123.3 3.2 %collective-permute-done.1 = bf16[3,2,2048]{2,1,0:T(2,128)(2,1)S(1)} collective-permute-done((bf16[3,2,2048]{2,1,0:T(2,128)(2,1)S(1)}, bf16[3,2,2048]{2,1,0:T(2,128)(2,1)S(1)}, u32[]{:S(2)}, u32[]{:S(2)}) %collective-permute-start.1) | collective-permute-done | bytes 24608 | tf_op jit(solution)/shard_map/ppermute | solution.py:21
  126.5 0.4 pad_maximum_fusion
  126.9 3.0 %multiply_reduce_fusion.2 = (f32[3,2048]{1,0:T(4,128)S(1)}, f32[3,2048]{1,0:T(4,128)S(1)}, f32[3,2048]{1,0:T(4,128)S(1)}, bf16[3,128,2048]{2,1,0:T(8,128)(2,1)}) fusion(f32[3,130,2048]{2,1,0:T(8,128)S(1)} %maximum_convert_fusion, f32[1,128,2048]{2,1,0:T(8,128)S(1)} %get-tuple-element.13, f32[1,128,2048]{2,1,0:T(8,128)S(1)} %get-tuple-element.12, ...), kind=kLoop, calls=%fused_computation.9 | loop fusion | flops 10991616 | bytes 20594688 | tf_op jit(solution)/shard_map/reduce_sum | solution.py:502
  130.0 0.1 maximum_multiply_fusion
  130.1 0.7 bitcast_bitcast_fusion.part_ref
  130.8 34.7 %tap_sums.1 = f32[16,16,128]{2,1,0:T(8,128)} custom-call(f32[16,16,128]{2,1,0:T(8,128)} %bitcast_bitcast_fusion.part_ref), custom_call_target="tpu_custom_call" | custom-call | tf_op jit(solution)/shard_map/tap_sums/pallas_call | solution.py:456
  165.5 0.9 copy.11
  166.4 0.7 reshape.19
  167.1 2.3 %copy.22 = f32[128,2048]{1,0:T(8,128)} copy(f32[128,2048]{1,0:T(8,128)} %get-tuple-element.27) | data formatting | bytes 2097152
  (14 shorter events, 0.2 us)
Async XLA Ops:
  7.2 26.4 %all-gather.2.cloned.1.call-start = ((), (), s32[]{:S(2)}) async-start(), calls=%async_computation | async-start | bytes 1572864 | tf_op jit(solution)/shard_map/all_gather | solution.py:487
  8.8 3.5 %collective-permute-start = (bf16[3,2,2048]{2,1,0:T(2,128)(2,1)S(1)}, bf16[3,2,2048]{2,1,0:T(2,128)(2,1)S(1)}, u32[]{:S(2)}, u32[]{:S(2)}) collective-permute-start(bf16[3,2,2048]{2,1,0:T(2,128)(2,1)S(1)} %slice.51), channel_id=1, source_target_pairs={{0,2},{2,4},{4,6},{6,8},{8,10},{10,12},{12,14},{14,16},{16,18},{18... | collective-permute-start | bytes 73736 | tf_op jit(solution)/shard_map/ppermute | solution.py:21
  47.8 71.8 %copy-start = (f32[3,128,2048]{2,1,0:T(8,128)S(1)}, f32[3,128,2048]{2,1,0:T(8,128)}, u32[]{:S(2)}) copy-start(f32[3,128,2048]{2,1,0:T(8,128)} %multiply_add_fusion) | copy-start | bytes 9437188
  119.6 1.6 copy-start.1
  119.6 1.8 %copy-start.2 = (f32[128,2048]{1,0:T(8,128)S(1)}, f32[128,2048]{1,0:T(8,128)}, u32[]{:S(2)}) copy-start(f32[128,2048]{1,0:T(8,128)} %get-tuple-element.6) | copy-start | bytes 3145732
  122.0 4.5 %collective-permute-start.1 = (bf16[3,2,2048]{2,1,0:T(2,128)(2,1)S(1)}, bf16[3,2,2048]{2,1,0:T(2,128)(2,1)S(1)}, u32[]{:S(2)}, u32[]{:S(2)}) collective-permute-start(bf16[3,2,2048]{2,1,0:T(2,128)(2,1)S(1)} %slice.104), channel_id=1, source_target_pairs={{2,0},{4,2},{6,4},{8,6},{10,8},{12,10},{14,12},{16,14},{18,16},{20... | collective-permute-start | bytes 73736 | tf_op jit(solution)/shard_map/ppermute | solution.py:21
Sparse Core Ops, SparseCore 0:
  9.5 23.9 all-gather.1

commit v2 on v0

--- a/solution.py
+++ b/solution.py
@@ -1,11 +1,18 @@
+import functools
 import math
 
 import jax
 import jax.numpy as jnp
+import numpy as np
 from jax import lax
+from jax.experimental import pallas as pl
+from jax.experimental.pallas import tpu as pltpu
 from jax.sharding import PartitionSpec as P
 
 HIGH = lax.Precision.HIGHEST
+MESH = pl.DeviceIdType.MESH
+FINE = 256
+TOP = 248.0 * 128.0 - 1.0
 
 
 def shifted(x, axis, by):
@@ -160,9 +167,477 @@
     return (inputs_grad.astype(jnp.bfloat16), raw * scale, short_grad)
 
 
+def log2(x):
+    return jnp.log(x) * (1.0 / math.log(2.0))
+
+
+def encode(x):
+    peak = jnp.maximum(jnp.max(jnp.abs(x), axis=0, keepdims=True), 1e-30)
+    power = jnp.ceil(log2(peak))
+    level = jnp.floor(jnp.abs(x) * (jnp.exp2(-power) * TOP) + 0.5)
+    level = jnp.minimum(level, TOP)
+    octave = jnp.floor(level * (1.0 / 128.0))
+    size = jnp.exp2(octave - 123.0) * (1.0 + (level - octave * 128.0) * (1.0 / 128.0))
+    return jnp.where(x < 0.0, -size, size).astype(jnp.bfloat16), power
+
+
+def decode(words, power):
+    words = words.astype(jnp.float32)
+    size = jnp.abs(words)
+    octave = jnp.floor(log2(size) + 0.0014)
+    part = jnp.floor(size * jnp.exp2(-octave) * 128.0 + 0.5)
+    level = octave * 128.0 + part + (123.0 * 128.0 - 128.0)
+    return jnp.where(words < 0.0, -level, level) * (jnp.exp2(power.astype(jnp.float32)) / TOP)
+
+
+def rows_of(powers):
+    row = lax.broadcasted_iota(jnp.int32, (16, powers[0].shape[1]), 0)
+    return jnp.where(row == 0, powers[0], powers[-1]).astype(jnp.bfloat16)
+
+
+def split(x):
+    high = x.astype(jnp.bfloat16)
+    return high, (x - high.astype(jnp.float32)).astype(jnp.bfloat16)
+
+
+def product3(m_high, m_low, x):
+    x_high, x_low = split(x)
+    dot = lambda a, b: jnp.dot(a, b, preferred_element_type=jnp.float32)
+    return dot(m_high, x_high) + (dot(m_low, x_high) + dot(m_high, x_low))
+
+
+def times_root(z, k, count, sign):
+    re, im = z
+    k = k % count
+    if 8 * k % count == 0:
+        turn = 8 * k // count
+        if turn % 2 == 0:
+            for _ in range(turn // 2):
+                re, im = (im, -re) if sign < 0 else (-im, re)
+            return re, im
+    c, s = math.cos(2 * math.pi * k / count), sign * math.sin(2 * math.pi * k / count)
+    if 8 * k % count == 0:
+        r = abs(c)
+        if (c > 0) == (s > 0):
+            out = (re - im) * r, (re + im) * r
+        else:
+            out = (re + im) * r, (im - re) * r
+        return out if c > 0 else (-out[0], -out[1])
+    return re * c - im * s, re * s + im * c
+
+
+def small_dft(z, sign):
+    count = len(z)
+    if count == 1:
+        return z
+    even, odd = small_dft(z[0::2], sign), small_dft(z[1::2], sign)
+    odd = [times_root(v, k, count, sign) for k, v in enumerate(odd)]
+    return [(a[0] + b[0], a[1] + b[1]) for a, b in zip(even, odd)] + [
+        (a[0] - b[0], a[1] - b[1]) for a, b in zip(even, odd)
+    ]
+
+
+def matrices(length):
+    radix = length // FINE
+    k = np.arange(FINE)[None, :, None] + 0.25
+    n = radix * np.arange(FINE)[None, None, :] + np.arange(radix)[:, None, None]
+    angle = -2.0 * np.pi * k * n / length
+    forward = np.concatenate([np.cos(angle), np.sin(angle)], axis=1).astype(np.float32)
+
+    def halves(m):
+        high = m.astype(jnp.bfloat16)
+        return np.stack([high, (m - high.astype(np.float32)).astype(jnp.bfloat16)])
+
+    return halves(forward), halves(np.ascontiguousarray(forward.transpose(0, 2, 1)))
+
+
+def greet():
+    me, count = lax.axis_index("ctx"), lax.axis_size("ctx")
+    line, lines = lax.axis_index("tp"), lax.axis_size("tp")
+    barrier = pltpu.get_barrier_semaphore()
+    for s in range(1, count):
+        peer = {"ctx": lax.rem(me + s, count)}
+        pl.semaphore_signal(barrier, inc=1, device_id=peer, device_id_type=MESH)
+    for s in range(1, lines):
+        peer = {"tp": lax.rem(line + s, lines)}
+        pl.semaphore_signal(barrier, inc=1, device_id=peer, device_id_type=MESH)
+    pl.semaphore_wait(barrier, count + lines - 2)
+
+
+def remote(src, dst, send_sem, recv_sem, peer):
+    return pltpu.make_async_remote_copy(
+        src_ref=src,
+        dst_ref=dst,
+        send_sem=send_sem,
+        recv_sem=recv_sem,
+        device_id=peer,
+        device_id_type=MESH,
+    )
+
+
+def operator_kernel(
+    count, lines, span, scale,
+    x_ref, sw_ref, taps_ref, w_hbm, go_ref, f_hbm, ft_hbm,
+    ig_ref, tg_ref, sg_ref,
+    w_ref, f_ref, ft_ref, go_all, ext, mix, gg, dm, xs, ys,
+    pair_out, pair_in, one_out, one_in, halo_out, halo_in, parts, parts_in, total,
+    local_sem, go_sem, halo_sem, send_sem, recv_sem,
+):
+    rows, width = taps_ref.shape
+    lanes = width // count
+    length = rows * count
+    radix = length // FINE
+    keep = span - 1
+    me, line = lax.axis_index("ctx"), lax.axis_index("tp")
+    group = max(1, FINE // lanes)
+    groups = count // group
+
+    def group_at(j):
+        return lax.rem(lax.div(me, group) + j, groups)
+
+    def w_load(j):
+        at = pl.ds(pl.multiple_of(group_at(j) * group * lanes, lanes), group * lanes)
+        return pltpu.make_async_copy(w_hbm.at[at], w_ref.at[at], local_sem.at[j])
+
+    f_loads = [
+        pltpu.make_async_copy(f_hbm, f_ref, local_sem.at[groups]),
+        pltpu.make_async_copy(ft_hbm, ft_ref, local_sem.at[groups + 1]),
+    ]
+    for j in range(groups):
+        w_load(j).start()
+    for load in f_loads:
+        load.start()
+
+    for b in range(3):
+        ext[b, 8:, :] = x_ref[b].astype(jnp.float32)
+        halo_out[0, b * keep : (b + 1) * keep, :] = ext[b, 8 + rows - keep :, :]
+    go_all[line] = go_ref[...]
+    parts[...] = jnp.zeros_like(parts)
+    greet()
+
+    def halo(way, peer):
+        return remote(
+            halo_out.at[way], halo_in.at[way], halo_sem.at[way, 0], halo_sem.at[way, 1],
+            {"ctx": peer},
+        )
+
+    def go_copy(owner, s, peer):
+        return remote(
+            go_ref, go_all.at[owner], go_sem.at[0, s], go_sem.at[1, s], {"tp": peer}
+        )
+
+    down = halo(0, lax.rem(me + 1, count))
+    down.start()
+    for s in range(1, lines):
+        go_copy(line, s, lax.rem(line + s, lines)).start()
+
+    def columns(d):
+        return pl.ds(pl.multiple_of(d * lanes, lanes), lanes)
+
+    def block_rows(d):
+        return pl.ds(pl.multiple_of(d * rows, rows), rows)
+
+    def sending(src, dst, phase, peer):
+        return remote(
+            src.at[peer], dst.at[me], send_sem.at[phase, peer], recv_sem.at[phase, me],
+            {"ctx": peer},
+        )
+
+    def landing(src, dst, phase, peer):
+        return remote(
+            src.at[peer], dst.at[peer], send_sem.at[phase, peer], recv_sem.at[phase, peer],
+            {"ctx": peer},
+        )
+
+    def fill(buf, d, values):
+        powers = []
+        for a, x in enumerate(values):
+            words, power = encode(x)
+            buf[d, pl.ds(a * rows, rows), :] = words
+            powers.append(power)
+        buf[d, pl.ds(len(values) * rows, 16), :] = rows_of(powers)
+
+    def read(src, dst, phase, s, many):
+        d = lax.rem(me + count - s, count)
+        if s:
+            landing(src, dst, phase, d).wait_recv()
+        block = src[d] if s == 0 else dst[d]
+        powers = block[many * rows :].astype(jnp.float32)
+        return d, [
+            (block[a * rows : (a + 1) * rows], powers[a : a + 1]) for a in range(many)
+        ]
+
+    order = list(range(1, count)) + [0]
+
+    down.wait_recv()
+    for b in range(3):
+        got = halo_in[0, b * keep : (b + 1) * keep, :]
+        ext[b, 8 - keep : 8, :] = jnp.where(me == 0, jnp.zeros_like(got), got)
+
+    def mixing(c):
+        at = columns(c)
+        for b in range(3):
+            value = jnp.zeros((rows, lanes), jnp.float32)
+            for j in range(span):
+                tap = sw_ref[b * span + j : b * span + j + 1, at]
+                value = value + tap * ext[b, pl.ds(8 - j, rows), at]
+            mix[b, :, at] = value
+
+    for s in order:
+        d = lax.rem(me + s, count)
+        mixing(d)
+        fill(pair_out.at[0], d, [taps_ref[:, columns(d)], mix[1, :, columns(d)] * mix[2, :, columns(d)]])
+        if s:
+            sending(pair_out.at[0], pair_in.at[0], 0, d).start()
+
+    for s in range(1, lines):
+        owner = lax.rem(line + lines - s, lines)
+        go_copy(owner, s, owner).wait_recv()
+    features = go_ref.shape[1]
+    for j in range(groups):
+        w_load(j).wait()
+        at = pl.ds(pl.multiple_of(group_at(j) * group * lanes, lanes), group * lanes)
+        value = jnp.zeros((rows, group * lanes), jnp.float32)
+        for t in range(lines):
+            value = value + lax.dot_general(
+                go_all[t],
+                w_ref[at, t * features : (t + 1) * features],
+                (((1,), (1,)), ((), ())),
+                preferred_element_type=jnp.float32,
+            )
+        gg[:, at] = value
+        for i in range(group):
+            d = group_at(j) * group + i
+            fill(one_out.at[0], d, [gg[:, columns(d)] * mix[0, :, columns(d)]])
+
+            @pl.when(d != me)
+            def _():
+                sending(one_out.at[0], one_in.at[0], 1, d).start()
+
+    def forward(first, last):
+        cols = pl.ds(first * lanes, (last - first) * lanes)
+        for n2 in range(radix):
+            x = [xs[a, pl.ds(n2, FINE, stride=radix), :] for a in range(first, last)]
+            x = x[0] if len(x) == 1 else jnp.concatenate(x, axis=1)
+            ys[n2, :, cols] = product3(f_ref[0, n2], f_ref[1, n2], x)
+
+    def inverse(first, last):
+        cols = pl.ds(first * lanes, (last - first) * lanes)
+        for n2 in range(radix):
+            x = product3(ft_ref[0, n2], ft_ref[1, n2], ys[n2, :, cols])
+            for a in range(first, last):
+                xs[a, pl.ds(n2, FINE, stride=radix), :] = x[
+                    :, (a - first) * lanes : (a - first + 1) * lanes
+                ]
+
+    def load_tile(row, a):
+        cols = pl.ds(a * lanes, lanes)
+        return [
+            (ys[n2, pl.ds(row, 8), cols], ys[n2, pl.ds(FINE + row, 8), cols])
+            for n2 in range(radix)
+        ]
+
+    def save_tile(row, a, z):
+        cols = pl.ds(a * lanes, lanes)
+        for n2, (re, im) in enumerate(z):
+            ys[n2, pl.ds(row, 8), cols] = re
+            ys[n2, pl.ds(FINE + row, 8), cols] = im
+
+    for s in range(count):
+        d, blocks = read(pair_out.at[0], pair_in.at[0], 0, s, 2)
+        for a in range(2):
+            xs[a, block_rows(d), :] = decode(*blocks[a])
+    for load in f_loads:
+        load.wait()
+    forward(0, 2)
+
+    def spectra(t, _):
+        row = pl.multiple_of(t * 8, 8)
+        for a in range(2):
+            save_tile(row, a, small_dft(load_tile(row, a), -1))
+        return 0
+
+    lax.fori_loop(0, FINE // 8, spectra, 0)
+
+    for s in range(count):
+        d, blocks = read(one_out.at[0], one_in.at[0], 1, s, 1)
+        xs[2, block_rows(d), :] = decode(*blocks[0])
+    forward(2, 3)
+
+    def products(t, _):
+        row = pl.multiple_of(t * 8, 8)
+        filt, prod = load_tile(row, 0), load_tile(row, 1)
+        grad = small_dft(load_tile(row, 2), -1)
+        joined = [[], [], []]
+        for (fr, fi), (pr, pi), (gr, gi) in zip(filt, prod, grad):
+            joined[0].append((fr * pr - fi * pi, fr * pi + fi * pr))
+            joined[1].append((fr * gr + fi * gi, fr * gi - fi * gr))
+            joined[2].append((pr * gr + pi * gi, pr * gi - pi * gr))
+        for a in range(3):
+            save_tile(row, a, small_dft(joined[a], 1))
+        return 0
+
+    lax.fori_loop(0, FINE // 8, products, 0)
+
+    inverse(0, 2)
+    for s in order:
+        d = lax.rem(me + s, count)
+        fill(pair_out.at[1], d, [xs[a, block_rows(d), :] for a in range(2)])
+        if s:
+            sending(pair_out.at[1], pair_in.at[1], 2, d).start()
+    inverse(2, 3)
+    for s in order:
+        d = lax.rem(me + s, count)
+        fill(one_out.at[1], d, [xs[2, block_rows(d), :]])
+        if s:
+            sending(one_out.at[1], one_in.at[1], 3, d).start()
+
+    factor = scale / length
+    for s in range(count):
+        d, blocks = read(pair_out.at[1], pair_in.at[1], 2, s, 2)
+        at = columns(d)
+        conv_out, dz = decode(*blocks[0]) * factor, decode(*blocks[1]) * factor
+        for b, value in enumerate((gg[:, at] * conv_out, dz * mix[2, :, at], dz * mix[1, :, at])):
+            dm[b, 0:rows, at] = value
+            halo_out[1, b * keep : (b + 1) * keep, at] = value[:keep]
+            for j in range(span):
+                parts[d, b * span + j : b * span + j + 1, :] = jnp.sum(
+                    value * ext[b, pl.ds(8 - j, rows), at], axis=0, keepdims=True
+                )
+        if s:
+            sending(parts, parts_in, 4, d).start()
+    up = halo(1, lax.rem(me + count - 1, count))
+    up.start()
+    value = parts[me]
+    for s in range(1, count):
+        d = lax.rem(me + count - s, count)
+        landing(parts, parts_in, 4, d).wait_recv()
+        value = value + parts_in[d]
+    total[...] = value * scale
+    sg_ref[me] = value * scale
+
+    def sharing(peer, slot):
+        return remote(
+            total, sg_ref.at[slot], send_sem.at[5, peer], recv_sem.at[5, slot], {"ctx": peer}
+        )
+
+    for s in range(1, count):
+        sharing(lax.rem(me + s, count), me).start()
+
+    up.wait_recv()
+    for b in range(3):
+        got = halo_in[1, b * keep : (b + 1) * keep, :]
+        dm[b, rows : rows + keep, :] = jnp.where(me == count - 1, jnp.zeros_like(got), got)
+
+    def finish(c, _):
+        at = columns(c)
+        for b in range(3):
+            value = jnp.zeros((rows, lanes), jnp.float32)
+            for j in range(span):
+                tap = sw_ref[b * span + j : b * span + j + 1, at]
+                value = value + tap * dm[b, pl.ds(j, rows), at]
+            ig_ref[b, :, at] = value.astype(jnp.bfloat16)
+        return 0
+
+    lax.fori_loop(0, count, finish, 0)
+    for s in range(count):
+        d, blocks = read(one_out.at[1], one_in.at[1], 3, s, 1)
+        tg_ref[:, columns(d)] = decode(*blocks[0]) * factor
+    for s in range(1, count):
+        d = lax.rem(me + count - s, count)
+        sharing(d, d).wait_recv()
+
+    down.wait_send()
+    up.wait_send()
+    for s in range(1, lines):
+        go_copy(line, s, lax.rem(line + s, lines)).wait_send()
+    for s in range(1, count):
+        d = lax.rem(me + s, count)
+        sending(pair_out.at[0], pair_in.at[0], 0, d).wait_send()
+        sending(one_out.at[0], one_in.at[0], 1, d).wait_send()
+        sending(pair_out.at[1], pair_in.at[1], 2, d).wait_send()
+        sending(one_out.at[1], one_in.at[1], 3, d).wait_send()
+        sending(parts, parts_in, 4, d).wait_send()
+        sharing(d, me).wait_send()
+
+
+def channel_shards(inputs, short_weight, taps, w_out, grad_out):
+    rows, width = taps.shape
+    span = short_weight.shape[1]
+    count, lines = lax.axis_size("ctx"), lax.axis_size("tp")
+    lanes, length = width // count, rows * count
+    radix, groups = length // FINE, count // max(1, FINE // lanes)
+    scale = 1.0 / math.sqrt(length)
+    forward, backward = matrices(length)
+    vmem, anywhere = pl.BlockSpec(memory_space=pltpu.VMEM), pl.BlockSpec(memory_space=pl.ANY)
+    f32, bf16 = jnp.float32, jnp.bfloat16
+    sums = (count, -(-3 * span // 8) * 8, lanes)
+    inputs_grad, taps_grad, short_grad = pl.pallas_call(
+        functools.partial(operator_kernel, count, lines, span, scale),
+        out_shape=[
+            jax.ShapeDtypeStruct(inputs.shape, bf16),
+            jax.ShapeDtypeStruct(taps.shape, f32),
+            jax.ShapeDtypeStruct(sums, f32),
+        ],
+        in_specs=[vmem, vmem, vmem, anywhere, vmem, anywhere, anywhere],
+        out_specs=[vmem] * 3,
+        scratch_shapes=[
+            pltpu.VMEM(w_out.shape, bf16),
+            pltpu.VMEM(forward.shape, bf16),
+            pltpu.VMEM(backward.shape, bf16),
+            pltpu.VMEM((lines,) + grad_out.shape, bf16),
+            pltpu.VMEM((3, rows + 8, width), f32),
+            pltpu.VMEM((3, rows, width), f32),
+            pltpu.VMEM((rows, width), f32),
+            pltpu.VMEM((3, rows + 8, width), f32),
+            pltpu.VMEM((3, length, lanes), f32),
+            pltpu.VMEM((radix, 2 * FINE, 3 * lanes), f32),
+            pltpu.VMEM((2, count, 2 * rows + 16, lanes), bf16),
+            pltpu.VMEM((2, count, 2 * rows + 16, lanes), bf16),
+            pltpu.VMEM((2, count, rows + 16, lanes), bf16),
+            pltpu.VMEM((2, count, rows + 16, lanes), bf16),
+            pltpu.VMEM((2, -(-3 * (span - 1) // 8) * 8, width), f32),
+            pltpu.VMEM((2, -(-3 * (span - 1) // 8) * 8, width), f32),
+            pltpu.VMEM(sums, f32),
+            pltpu.VMEM(sums, f32),
+            pltpu.VMEM(sums[1:], f32),
+            pltpu.SemaphoreType.DMA((groups + 2,)),
+            pltpu.SemaphoreType.DMA((2, lines)),
+            pltpu.SemaphoreType.DMA((2, 2)),
+            pltpu.SemaphoreType.DMA((6, count)),
+            pltpu.SemaphoreType.DMA((6, count)),
+        ],
+        compiler_params=pltpu.CompilerParams(
+            collective_id=0, has_side_effects=True, vmem_limit_bytes=62 * 2**20
+        ),
+        cost_estimate=pl.CostEstimate(
+            flops=2 * rows * width * w_out.shape[1], bytes_accessed=2 * w_out.size, transcendentals=0
+        ),
+        name="operator_backward",
+    )(
+        inputs,
+        short_weight.reshape(3 * span, width),
+        taps,
+        w_out,
+        grad_out,
+        jnp.asarray(forward),
+        jnp.asarray(backward),
+    )
+    short_grad = short_grad.transpose(1, 0, 2).reshape(sums[1], width)[: 3 * span]
+    return inputs_grad, taps_grad, short_grad.reshape(3, span, width)
+
+
+def any_shards(inputs, short_weight, taps, w_out, grad_out):
+    rows, width = taps.shape
+    count = lax.axis_size("ctx")
+    whole_tiles = rows % 16 == 0 and width % (128 * count) == 0 and rows * count == 8 * FINE
+    plan = channel_shards if whole_tiles else shards
+    return plan(inputs, short_weight, taps, w_out, grad_out)
+
+
 def solution(mesh):
     return jax.shard_map(
-        shards,
+        any_shards,
         mesh=mesh,
         in_specs=(
             P(None, "ctx", "tp"),

time: 1120 us -> 111 us (0.10)
  blocking collectives: 401 us -> 0 us
  waiting for transfers between devices: 389 us -> 0 us
  matrix products: 121 us -> 0 us
  local copies, waits for them, and re-layouts: 121 us -> 6.97 us
  Pallas kernels: 0 us -> 103 us
  other arithmetic: 39.5 us -> 0 us
  starting transfers between devices: 25.5 us -> 0 us
  between operations: 15 us -> 0.65 us
    all_to_all x2 -> x0, blocking collectives: 401 us -> none  [the longest x1 325 us: shards(): lax.all_to_all(back, 'ctx', split_axis=3, concat_axis=2, tiled=True)]
    all_to_all x2 -> x0, waiting for transfers between devices: 283 us -> none  [the longest x1 223 us: shards(): lax.all_to_all(columns, 'ctx', split_axis=2, concat_axis=3, tiled=True)]
    dot_general x13 -> x0, matrix products: 121 us -> none  [the longest x1 12.7 us: shards(): lax.dot_general(lax.all_gather(grad_out, 'tp', axis=1, tiled=True), colum...]
    pallas_call x0 -> x1, Pallas kernels: none -> 103 us  [channel_shards(): pl.pallas_call(functools.partial(operator_kernel, count, lines, span, sca...]
    psum x1 -> x0, waiting for transfers between devices: 87.2 us -> none  [shards(): short_grad = lax.psum(jnp.stack(sums, axis=1), 'ctx') * scale]
    another operation x3 -> x0, local copies, waits for them, and re-layouts: 37.5 us -> none  [the longest x1 19.2 us: inverse_two(): jnp.stack([back_re * tw_re - back_im * tw_im, back_re * tw_im + back_im *...]
    slice x7 -> x1, local copies, waits for them, and re-layouts: 35.1 us -> 1.02 us  [channel_shards(): short_grad.transpose(1, 0, 2).reshape(sums[1], width)[:3 * span]]
    all_to_all x2 -> x0, local copies, waits for them, and re-layouts: 27.6 us -> none  [the longest x1 16.3 us: shards(): lax.all_to_all(back, 'ctx', split_axis=3, concat_axis=2, tiled=True)]
  transfers between devices with their start and end apart: 6 -> 0, of which waited for: 5 -> 0; matrix products, arithmetic and copies ran while one was open for 1% -> 0% of each run, Pallas kernels for 0% -> 0%
where the time goes in v2:
time: 111 us
  Pallas kernels  103 us (93%)
  local copies, waits for them, and re-layouts  6.97 us (6%)
    pallas_call x1, Pallas kernels, channel_shards(): pl.pallas_call(functools.partial(operator_kernel, count, lines, span, sca...  103 us
    unnamed x4, local copies, waits for them, and re-layouts  3.7 us

profile of v2, /device:TPU:0, one launch (start us, length us, event | category | flops | bytes accessed | tf_op | source)
XLA Modules:
  0.0 110.8 jit_solution(5667031598885904452)
XLA Ops:
  0.6 1.6 %reshape.15.sw_ref = f32[9,2048]{1,0:T(8,128)} reshape(f32[3,3,2048]{2,1,0:T(4,128)} %param.8) | data formatting | bytes 147456 | tf_op jit(solution)/shard_map/reshape | solution.py:619
  2.2 103.2 %operator_backward.1 = (bf16[3,128,2048]{2,1,0:T(8,128)(2,1)}, f32[128,2048]{1,0:T(8,128)}, f32[16,16,128]{2,1,0:T(8,128)}) custom-call(bf16[3,128,2048]{2,1,0:T(8,128)(2,1)} %x_ref.1, f32[9,2048]{1,0:T(8,128)} %reshape.15.sw_ref, f32[128,2048]{1,0:T(8,128)} %taps_ref.1, bf16[2048,4096]{1,0:T(8,128)(2,1)} %w_hbm.1, bf16[128,2048]{1,0:T(8,128)(2,1)} %go_ref.1, ...), custom_call_target="tpu_custom_call" | custom-call | flops 2147483648 | bytes 16777216 | tf_op jit(solution)/shard_map/operator_backward/pallas_call | solution.py:575
  105.4 0.0 copy-start
  105.4 1.0 copy.10
  106.4 0.7 reshape.16
  107.1 2.7 %copy.13 = bf16[3,128,2048]{2,1,0:T(8,128)(2,1)} copy(bf16[3,128,2048]{2,1,0:T(8,128)(2,1)} %get-tuple-element.12) | data formatting | bytes 3145728
  109.8 0.0 copy-done
  109.8 1.0 copy.14
Async XLA Ops:
  105.4 4.4 %copy-start = (f32[128,2048]{1,0:T(8,128)S(1)}, f32[128,2048]{1,0:T(8,128)}, u32[]{:S(2)}) copy-start(f32[128,2048]{1,0:T(8,128)} %get-tuple-element.13) | copy-start | bytes 3145732

commit v3 on v2

--- a/solution.py
+++ b/solution.py
@@ -190,11 +190,6 @@
     return jnp.where(words < 0.0, -level, level) * (jnp.exp2(power.astype(jnp.float32)) / TOP)
 
 
-def rows_of(powers):
-    row = lax.broadcasted_iota(jnp.int32, (16, powers[0].shape[1]), 0)
-    return jnp.where(row == 0, powers[0], powers[-1]).astype(jnp.bfloat16)
-
-
 def split(x):
     high = x.astype(jnp.bfloat16)
     return high, (x - high.astype(jnp.float32)).astype(jnp.bfloat16)
@@ -280,7 +275,7 @@
     x_ref, sw_ref, taps_ref, w_hbm, go_ref, f_hbm, ft_hbm,
     ig_ref, tg_ref, sg_ref,
     w_ref, f_ref, ft_ref, go_all, ext, mix, gg, dm, xs, ys,
-    pair_out, pair_in, one_out, one_in, halo_out, halo_in, parts, parts_in, total,
+    out_buf, in_buf, halo_out, halo_in, parts, parts_in, total,
     local_sem, go_sem, halo_sem, send_sem, recv_sem,
 ):
     rows, width = taps_ref.shape
@@ -349,25 +344,29 @@
             {"ctx": peer},
         )
 
-    def fill(buf, d, values):
-        powers = []
-        for a, x in enumerate(values):
-            words, power = encode(x)
-            buf[d, pl.ds(a * rows, rows), :] = words
-            powers.append(power)
-        buf[d, pl.ds(len(values) * rows, 16), :] = rows_of(powers)
-
-    def read(src, dst, phase, s, many):
+    def block_send(phase, d):
+        return sending(out_buf.at[phase], in_buf.at[phase], phase, d)
+
+    def fill(phase, d, value):
+        words, power = encode(value)
+        out_buf[phase, d, 0:rows, :] = words
+        out_buf[phase, d, pl.ds(rows, 16), :] = jnp.broadcast_to(power, (16, lanes)).astype(
+            jnp.bfloat16
+        )
+
+    def read(phase, s):
         d = lax.rem(me + count - s, count)
         if s:
-            landing(src, dst, phase, d).wait_recv()
-        block = src[d] if s == 0 else dst[d]
-        powers = block[many * rows :].astype(jnp.float32)
-        return d, [
-            (block[a * rows : (a + 1) * rows], powers[a : a + 1]) for a in range(many)
-        ]
-
-    order = list(range(1, count)) + [0]
+            landing(out_buf.at[phase], in_buf.at[phase], phase, d).wait_recv()
+        block = out_buf[phase, d] if s == 0 else in_buf[phase, d]
+        return d, decode(block[:rows], block[rows:].astype(jnp.float32)[0:1])
+
+    far = sorted(range(1, count), key=lambda s: -min(s, count - s))
+    for s in far + [0]:
+        d = lax.rem(me + s, count)
+        fill(0, d, taps_ref[:, columns(d)])
+        if s:
+            block_send(0, d).start()
 
     down.wait_recv()
     for b in range(3):
@@ -379,16 +378,16 @@
         for b in range(3):
             value = jnp.zeros((rows, lanes), jnp.float32)
             for j in range(span):
-                tap = sw_ref[b * span + j : b * span + j + 1, at]
+                tap = sw_ref[b, j : j + 1, at]
                 value = value + tap * ext[b, pl.ds(8 - j, rows), at]
             mix[b, :, at] = value
 
-    for s in order:
+    for s in far + [0]:
         d = lax.rem(me + s, count)
         mixing(d)
-        fill(pair_out.at[0], d, [taps_ref[:, columns(d)], mix[1, :, columns(d)] * mix[2, :, columns(d)]])
+        fill(1, d, mix[1, :, columns(d)] * mix[2, :, columns(d)])
         if s:
-            sending(pair_out.at[0], pair_in.at[0], 0, d).start()
+            block_send(1, d).start()
 
     for s in range(1, lines):
         owner = lax.rem(line + lines - s, lines)
@@ -408,11 +407,11 @@
         gg[:, at] = value
         for i in range(group):
             d = group_at(j) * group + i
-            fill(one_out.at[0], d, [gg[:, columns(d)] * mix[0, :, columns(d)]])
+            fill(2, d, gg[:, columns(d)] * mix[0, :, columns(d)])
 
             @pl.when(d != me)
             def _():
-                sending(one_out.at[0], one_in.at[0], 1, d).start()
+                block_send(2, d).start()
 
     def forward(first, last):
         cols = pl.ds(first * lanes, (last - first) * lanes)
@@ -443,82 +442,90 @@
             ys[n2, pl.ds(row, 8), cols] = re
             ys[n2, pl.ds(FINE + row, 8), cols] = im
 
-    for s in range(count):
-        d, blocks = read(pair_out.at[0], pair_in.at[0], 0, s, 2)
-        for a in range(2):
-            xs[a, block_rows(d), :] = decode(*blocks[a])
+    def collect(phase, a):
+        for s in [0] + far:
+            d, value = read(phase, s)
+            xs[a, block_rows(d), :] = value
+
+    def give_back(phase, a):
+        inverse(a, a + 1)
+        for s in far + [0]:
+            d = lax.rem(me + s, count)
+            fill(phase, d, xs[a, block_rows(d), :])
+            if s:
+                block_send(phase, d).start()
+
+    def multiply(p, q):
+        return [(a * c - b * d, a * d + b * c) for (a, b), (c, d) in zip(p, q)]
+
+    def correlate(p, q):
+        return [(a * c + b * d, a * d - b * c) for (a, b), (c, d) in zip(p, q)]
+
+    collect(0, 0)
+    collect(1, 1)
     for load in f_loads:
         load.wait()
     forward(0, 2)
 
-    def spectra(t, _):
+    def early(t, _):
         row = pl.multiple_of(t * 8, 8)
+        specs = [small_dft(load_tile(row, a), -1) for a in range(2)]
         for a in range(2):
-            save_tile(row, a, small_dft(load_tile(row, a), -1))
+            save_tile(row, a, specs[a])
+        save_tile(row, 2, small_dft(multiply(*specs), 1))
         return 0
 
-    lax.fori_loop(0, FINE // 8, spectra, 0)
-
-    for s in range(count):
-        d, blocks = read(one_out.at[0], one_in.at[0], 1, s, 1)
-        xs[2, block_rows(d), :] = decode(*blocks[0])
+    lax.fori_loop(0, FINE // 8, early, 0)
+    give_back(3, 2)
+    collect(2, 2)
     forward(2, 3)
 
-    def products(t, _):
+    def late(t, _):
         row = pl.multiple_of(t * 8, 8)
-        filt, prod = load_tile(row, 0), load_tile(row, 1)
         grad = small_dft(load_tile(row, 2), -1)
-        joined = [[], [], []]
-        for (fr, fi), (pr, pi), (gr, gi) in zip(filt, prod, grad):
-            joined[0].append((fr * pr - fi * pi, fr * pi + fi * pr))
-            joined[1].append((fr * gr + fi * gi, fr * gi - fi * gr))
-            joined[2].append((pr * gr + pi * gi, pr * gi - pi * gr))
-        for a in range(3):
-            save_tile(row, a, small_dft(joined[a], 1))
+        for a in range(2):
+            save_tile(row, a, small_dft(correlate(load_tile(row, a), grad), 1))
         return 0
 
-    lax.fori_loop(0, FINE // 8, products, 0)
-
-    inverse(0, 2)
-    for s in order:
-        d = lax.rem(me + s, count)
-        fill(pair_out.at[1], d, [xs[a, block_rows(d), :] for a in range(2)])
+    lax.fori_loop(0, FINE // 8, late, 0)
+    give_back(4, 0)
+    give_back(5, 1)
+
+    factor = scale / length
+
+    def mixed_grad(b, d, value):
+        at = columns(d)
+        dm[b, 0:rows, at] = value
+        halo_out[1, b * keep : (b + 1) * keep, at] = value[:keep]
+        for j in range(span):
+            parts[d, b * span + j : b * span + j + 1, :] = jnp.sum(
+                value * ext[b, pl.ds(8 - j, rows), at], axis=0, keepdims=True
+            )
+
+    for s in [0] + far:
+        d, value = read(3, s)
+        mixed_grad(0, d, gg[:, columns(d)] * (value * factor))
+    for s in [0] + far:
+        d, value = read(4, s)
+        value = value * factor
+        mixed_grad(1, d, value * mix[2, :, columns(d)])
+        mixed_grad(2, d, value * mix[1, :, columns(d)])
         if s:
-            sending(pair_out.at[1], pair_in.at[1], 2, d).start()
-    inverse(2, 3)
-    for s in order:
-        d = lax.rem(me + s, count)
-        fill(one_out.at[1], d, [xs[2, block_rows(d), :]])
-        if s:
-            sending(one_out.at[1], one_in.at[1], 3, d).start()
-
-    factor = scale / length
-    for s in range(count):
-        d, blocks = read(pair_out.at[1], pair_in.at[1], 2, s, 2)
-        at = columns(d)
-        conv_out, dz = decode(*blocks[0]) * factor, decode(*blocks[1]) * factor
-        for b, value in enumerate((gg[:, at] * conv_out, dz * mix[2, :, at], dz * mix[1, :, at])):
-            dm[b, 0:rows, at] = value
-            halo_out[1, b * keep : (b + 1) * keep, at] = value[:keep]
-            for j in range(span):
-                parts[d, b * span + j : b * span + j + 1, :] = jnp.sum(
-                    value * ext[b, pl.ds(8 - j, rows), at], axis=0, keepdims=True
-                )
-        if s:
-            sending(parts, parts_in, 4, d).start()
+            sending(parts, parts_in, 6, d).start()
     up = halo(1, lax.rem(me + count - 1, count))
     up.start()
     value = parts[me]
     for s in range(1, count):
         d = lax.rem(me + count - s, count)
-        landing(parts, parts_in, 4, d).wait_recv()
+        landing(parts, parts_in, 6, d).wait_recv()
         value = value + parts_in[d]
     total[...] = value * scale
-    sg_ref[me] = value * scale
+    sg_ref[:, columns(me)] = value * scale
 
     def sharing(peer, slot):
         return remote(
-            total, sg_ref.at[slot], send_sem.at[5, peer], recv_sem.at[5, slot], {"ctx": peer}
+            total, sg_ref.at[:, columns(slot)], send_sem.at[7, peer], recv_sem.at[7, slot],
+            {"ctx": peer},
         )
 
     for s in range(1, count):
@@ -534,15 +541,15 @@
         for b in range(3):
             value = jnp.zeros((rows, lanes), jnp.float32)
             for j in range(span):
-                tap = sw_ref[b * span + j : b * span + j + 1, at]
+                tap = sw_ref[b, j : j + 1, at]
                 value = value + tap * dm[b, pl.ds(j, rows), at]
             ig_ref[b, :, at] = value.astype(jnp.bfloat16)
         return 0
 
     lax.fori_loop(0, count, finish, 0)
-    for s in range(count):
-        d, blocks = read(one_out.at[1], one_in.at[1], 3, s, 1)
-        tg_ref[:, columns(d)] = decode(*blocks[0]) * factor
+    for s in [0] + far:
+        d, value = read(5, s)
+        tg_ref[:, columns(d)] = value * factor
     for s in range(1, count):
         d = lax.rem(me + count - s, count)
         sharing(d, d).wait_recv()
@@ -553,11 +560,9 @@
         go_copy(line, s, lax.rem(line + s, lines)).wait_send()
     for s in range(1, count):
         d = lax.rem(me + s, count)
-        sending(pair_out.at[0], pair_in.at[0], 0, d).wait_send()
-        sending(one_out.at[0], one_in.at[0], 1, d).wait_send()
-        sending(pair_out.at[1], pair_in.at[1], 2, d).wait_send()
-        sending(one_out.at[1], one_in.at[1], 3, d).wait_send()
-        sending(parts, parts_in, 4, d).wait_send()
+        for phase in range(6):
+            block_send(phase, d).wait_send()
+        sending(parts, parts_in, 6, d).wait_send()
         sharing(d, me).wait_send()
 
 
@@ -577,7 +582,7 @@
         out_shape=[
             jax.ShapeDtypeStruct(inputs.shape, bf16),
             jax.ShapeDtypeStruct(taps.shape, f32),
-            jax.ShapeDtypeStruct(sums, f32),
+            jax.ShapeDtypeStruct((sums[1], width), f32),
         ],
         in_specs=[vmem, vmem, vmem, anywhere, vmem, anywhere, anywhere],
         out_specs=[vmem] * 3,
@@ -592,10 +597,8 @@
             pltpu.VMEM((3, rows + 8, width), f32),
             pltpu.VMEM((3, length, lanes), f32),
             pltpu.VMEM((radix, 2 * FINE, 3 * lanes), f32),
-            pltpu.VMEM((2, count, 2 * rows + 16, lanes), bf16),
-            pltpu.VMEM((2, count, 2 * rows + 16, lanes), bf16),
-            pltpu.VMEM((2, count, rows + 16, lanes), bf16),
-            pltpu.VMEM((2, count, rows + 16, lanes), bf16),
+            pltpu.VMEM((6, count, rows + 16, lanes), bf16),
+            pltpu.VMEM((6, count, rows + 16, lanes), bf16),
             pltpu.VMEM((2, -(-3 * (span - 1) // 8) * 8, width), f32),
             pltpu.VMEM((2, -(-3 * (span - 1) // 8) * 8, width), f32),
             pltpu.VMEM(sums, f32),
@@ -604,8 +607,8 @@
             pltpu.SemaphoreType.DMA((groups + 2,)),
             pltpu.SemaphoreType.DMA((2, lines)),
             pltpu.SemaphoreType.DMA((2, 2)),
-            pltpu.SemaphoreType.DMA((6, count)),
-            pltpu.SemaphoreType.DMA((6, count)),
+            pltpu.SemaphoreType.DMA((8, count)),
+            pltpu.SemaphoreType.DMA((8, count)),
         ],
         compiler_params=pltpu.CompilerParams(
             collective_id=0, has_side_effects=True, vmem_limit_bytes=62 * 2**20
@@ -616,15 +619,14 @@
         name="operator_backward",
     )(
         inputs,
-        short_weight.reshape(3 * span, width),
+        short_weight,
         taps,
         w_out,
         grad_out,
         jnp.asarray(forward),
         jnp.asarray(backward),
     )
-    short_grad = short_grad.transpose(1, 0, 2).reshape(sums[1], width)[: 3 * span]
-    return inputs_grad, taps_grad, short_grad.reshape(3, span, width)
+    return inputs_grad, taps_grad, short_grad[: 3 * span].reshape(3, span, width)
 
 
 def any_shards(inputs, short_weight, taps, w_out, grad_out):

time: 111 us -> 105 us (0.946)
  Pallas kernels: 103 us -> 98 us
    pallas_call x1, Pallas kernels: 103 us -> 98 us  [channel_shards(): pl.pallas_call(functools.partial(operator_kernel, count, lines, span, sca...]
    unnamed x4 -> x2, local copies, waits for them, and re-layouts: 3.7 us -> 5.02 us
    reshape x2 -> x1, local copies, waits for them, and re-layouts: 2.26 us -> 1.58 us  [channel_shards(): short_grad[:3 * span].reshape(3, span, width)]
where the time goes in v3:
time: 105 us
  Pallas kernels  98 us (93%)
  local copies, waits for them, and re-layouts  6.6 us (6%)
    pallas_call x1, Pallas kernels, channel_shards(): pl.pallas_call(functools.partial(operator_kernel, count, lines, span, sca...  98 us
    unnamed x2, local copies, waits for them, and re-layouts  5.02 us

profile of v3, /device:TPU:0, one launch (start us, length us, event | category | flops | bytes accessed | tf_op | source)
XLA Modules:
  0.0 105.3 jit_solution(1429804629754194831)
XLA Ops:
  0.6 98.0 %operator_backward.1 = (bf16[3,128,2048]{2,1,0:T(8,128)(2,1)}, f32[128,2048]{1,0:T(8,128)}, f32[16,2048]{1,0:T(8,128)}) custom-call(bf16[3,128,2048]{2,1,0:T(8,128)(2,1)} %x_ref.1, f32[3,3,2048]{2,1,0:T(4,128)} %sw_ref.1, f32[128,2048]{1,0:T(8,128)} %taps_ref.1, bf16[2048,4096]{1,0:T(8,128)(2,1)} %w_hbm.1, bf16[128,2048]{1,0:T(8,128)(2,1)} %go_ref.1, ...), custom_call_target="tpu_custom_call" | custom-call | flops 2147483648 | bytes 16777216 | tf_op jit(solution)/shard_map/operator_backward/pallas_call | solution.py:580
  98.7 1.6 %reshape.9 = f32[3,3,2048]{2,1,0:T(4,128)} reshape(f32[9,2048]{1,0:T(8,128)} %bitcast.1) | data formatting | bytes 147456 | tf_op jit(solution)/shard_map/reshape | solution.py:629
  100.3 2.7 %copy.12 = bf16[3,128,2048]{2,1,0:T(8,128)(2,1)} copy(bf16[3,128,2048]{2,1,0:T(8,128)(2,1)} %get-tuple-element.12) | data formatting | bytes 3145728
  103.0 2.3 %copy.13 = f32[128,2048]{1,0:T(8,128)} copy(f32[128,2048]{1,0:T(8,128)} %get-tuple-element.13) | data formatting | bytes 2097152
